TPU v7x, 32 devices: a whole 2x2x4 slice. The times are simulated.
32 devices in a mesh: pool: 8 (over y, x, core), tp: 4 (over z).
Axes of the slice: x: 2, y: 2, z: 4, core: 2. Of those that a mesh axis runs over, the one named last changes fastest.
Arguments:
- turn_query: bfloat16 [4096, 2048], P('pool', 'tp'), may hold values from -16 to 16
- turn_key: bfloat16 [4096, 512], P('pool', 'tp'), may hold values from -16 to 16, as said below
- turn_value: bfloat16 [4096, 512], P('pool', 'tp'), may hold values from -6 to 6
- pool_keys: bfloat16 [512, 128, 512], P('pool', None, 'tp'), may hold values from -16 to 16, as said below
- pool_values: bfloat16 [512, 128, 512], P('pool', None, 'tp'), may hold values from -6 to 6
- seat_session: int32 [16], replicated, may hold values from 0 to 15, as said below
- history_len: int32 [16], replicated, may hold values from 1 to 4096, as said below
- block_map: int32 [16, 32], replicated, may hold values from 0 to 511, as said below
- out_weight: bfloat16 [2048, 8192], P('tp', 'pool'), may hold values from -0.1875 to 0.1875
Outputs:
- layer_out: bfloat16 [4096, 8192], P('pool', 'tp')
Inputs may be any that keep to these rules, and one draw needn't show every extreme that they name: `seat_session`: A permutation of the sessions. `history_len`: the sessions of one owner, chosen afresh in every draw, have length 4096. Every slot of the pool is named exactly once. Call block j of session s live when j * 128 < history_len[s]; the slot's pool index is block_map[s, j] // 64. The live blocks of one pool index that belong to the sessions of one owner number at most 8; some owner receives exactly 8 from every pool index. `turn_key`: Real-valued keys. `pool_keys`: Real-valued keys; slots not named by a live block hold values that are never read.
All inputs are finite; a program needn't handle non-finite values.
Results may differ from a plain program's by a relative error of at most 0.019.
Values may be sent and summed in bfloat16 or wider, within the bound.
A program may use at most 128 MiB of HBM per device.

v0:
```python
import math

import jax
import jax.numpy as jnp
from jax import lax
from jax.sharding import PartitionSpec as P

rope_base = 1000000.0


def rotate(values, positions):
    half_dim = values.shape[-1] // 2
    freq_index = jnp.arange(half_dim, dtype=jnp.float32)
    inverse = rope_base ** (-2.0 * freq_index / values.shape[-1])
    angles = positions.astype(jnp.float32)[:, None, None] * inverse[None, None, :]
    cosine = jnp.cos(angles)
    sine_part = jnp.sin(angles)
    lower_half = values[..., :half_dim]
    upper_half = values[..., half_dim:]
    return jnp.concatenate(
        [
            lower_half * cosine - upper_half * sine_part,
            upper_half * cosine + lower_half * sine_part,
        ],
        axis=-1,
    )


def local(
    turn_query,
    turn_key,
    turn_value,
    pool_keys,
    pool_values,
    seat_session,
    history_len,
    block_map,
    out_weight,
):
    pooled_count = lax.axis_size("pool")
    current_index = lax.axis_index("pool")
    blocks_here = pool_keys.shape[0]
    rows_per_block = pool_keys.shape[1]
    head_dim = pool_keys.shape[2]
    block_count = block_map.shape[1]
    per_owner = seat_session.shape[0] // pooled_count
    capacity = per_owner * block_count // pooled_count
    element_count = per_owner * block_count
    turn_len = turn_query.shape[0] // per_owner
    group_size = turn_query.shape[1] // head_dim
    span_len = block_count * rows_per_block
    scaling = 1.0 / math.sqrt(head_dim)
    seat_length = history_len[seat_session]
    seat_map = block_map[seat_session]
    seats_per_device = (seat_map // blocks_here).reshape(pooled_count, element_count)
    seat_slot = (seat_map % blocks_here).reshape(pooled_count, element_count)
    block_numbers = jnp.arange(block_count, dtype=jnp.int32)
    alive_flags = (block_numbers[None, :] * rows_per_block < seat_length[:, None]).reshape(
        pooled_count, element_count
    )
    departing_rows = alive_flags & (seats_per_device == current_index)
    send_rank = jnp.cumsum(departing_rows.astype(jnp.int32), axis=1) - 1
    selected = departing_rows[:, None, :] & (
        send_rank[:, None, :] == jnp.arange(capacity, dtype=jnp.int32)[None, :, None]
    )
    slot_table = jnp.sum(jnp.where(selected, seat_slot[:, None, :], 0), axis=2).reshape(
        pooled_count * capacity
    )
    send_keys = pool_keys[slot_table]
    send_vals = pool_values[slot_table]
    own_lengths = lax.dynamic_slice_in_dim(seat_length, current_index * per_owner, per_owner, 0)
    token_ids = jnp.arange(turn_len, dtype=jnp.int32)
    causal = jnp.tile(token_ids[None, :] <= token_ids[:, None], (group_size, 1))

    def prepare_turn(seat_number):
        length = own_lengths[seat_number]
        row_lo = seat_number * turn_len
        turn_pos = length + token_ids
        queries = turn_query[row_lo : row_lo + turn_len].reshape(turn_len, group_size, head_dim)
        roped_query = rotate(queries.astype(jnp.float32), turn_pos).astype(jnp.bfloat16)
        roped_query = jnp.transpose(roped_query, (1, 0, 2)).reshape(group_size * turn_len, head_dim)
        new_keys = turn_key[row_lo : row_lo + turn_len].reshape(turn_len, 1, head_dim)
        roped_new = (
            rotate(new_keys.astype(jnp.float32), turn_pos)
            .astype(jnp.bfloat16)
            .reshape(turn_len, head_dim)
        )
        own_scores = (
            jnp.einsum("qd,kd->qk", roped_query, roped_new, preferred_element_type=jnp.float32)
            * scaling
        )
        own_scores = jnp.where(causal, own_scores, -jnp.inf)
        return (roped_query, own_scores)

    prepared = []
    arrived_keys, arrived_vals = (
        lax.all_to_all(send_keys, "pool", split_axis=0, concat_axis=0, tiled=True),
        lax.all_to_all(send_vals, "pool", split_axis=0, concat_axis=0, tiled=True),
    )
    prepared = [prepare_turn(seat_number) for seat_number in range(per_owner)]
    home_dev = lax.dynamic_slice_in_dim(seats_per_device, current_index, 1, 0)[0]
    resident_alive = lax.dynamic_slice_in_dim(alive_flags, current_index, 1, 0)[0]
    sources = jnp.arange(pooled_count, dtype=jnp.int32)[:, None]
    arriving = resident_alive[None, :] & (home_dev[None, :] == sources)
    rank_table = jnp.cumsum(arriving.astype(jnp.int32), axis=1) - 1
    arrive_rank = jnp.sum(jnp.where(arriving, rank_table, 0), axis=0)
    recv_index = jnp.where(resident_alive, home_dev * capacity + arrive_rank, 0)
    hist_keys = arrived_keys[recv_index].reshape(per_owner, span_len, head_dim)
    hist_vals = arrived_vals[recv_index].reshape(per_owner, span_len, head_dim)
    hist_pos = jnp.arange(span_len, dtype=jnp.int32)
    outputs = []
    for seat_number in range(per_owner):
        roped_query, own_scores = prepared[seat_number]
        length = own_lengths[seat_number]
        row_lo = seat_number * turn_len
        stored = hist_keys[seat_number].reshape(span_len, 1, head_dim)
        roped_hist = (
            rotate(stored.astype(jnp.float32), hist_pos)
            .astype(jnp.bfloat16)
            .reshape(span_len, head_dim)
        )
        far_scores = (
            jnp.einsum("qd,kd->qk", roped_query, roped_hist, preferred_element_type=jnp.float32)
            * scaling
        )
        far_scores = jnp.where((hist_pos < length)[None, :], far_scores, -jnp.inf)
        row_top = jnp.maximum(
            jnp.max(far_scores, axis=1, keepdims=True), jnp.max(own_scores, axis=1, keepdims=True)
        )
        far_weight = jnp.exp(far_scores - row_top)
        own_weight = jnp.exp(own_scores - row_top)
        denominator = jnp.sum(far_weight, axis=1, keepdims=True) + jnp.sum(
            own_weight, axis=1, keepdims=True
        )
        weighted = jnp.dot(
            far_weight.astype(jnp.bfloat16),
            hist_vals[seat_number],
            preferred_element_type=jnp.float32,
        )
        weighted = weighted + jnp.dot(
            own_weight.astype(jnp.bfloat16),
            turn_value[row_lo : row_lo + turn_len],
            preferred_element_type=jnp.float32,
        )
        head_rows = (
            (weighted / denominator).astype(jnp.bfloat16).reshape(group_size, turn_len, head_dim)
        )
        outputs.append(jnp.transpose(head_rows, (1, 0, 2)).reshape(turn_len, group_size * head_dim))
    attended = jnp.concatenate(outputs, axis=0)
    partial_value = jnp.dot(
        attended,
        lax.all_gather(out_weight, "pool", axis=1, tiled=True),
        preferred_element_type=jnp.float32,
    )
    partial_value = partial_value.astype(jnp.bfloat16).astype(jnp.float32)
    summed = lax.psum_scatter(
        partial_value.astype(jnp.bfloat16), "tp", scatter_dimension=1, tiled=True
    )
    return summed


def solution(mesh):
    return jax.shard_map(
        local,
        mesh=mesh,
        in_specs=(
            P("pool", "tp"),
            P("pool", "tp"),
            P("pool", "tp"),
            P("pool", None, "tp"),
            P("pool", None, "tp"),
            P(),
            P(),
            P(),
            P("tp", "pool"),
        ),
        out_specs=P("pool", "tp"),
        check_vma=False,
    )
```

profile of v0, /device:TPU:0, one launch (start us, length us, event | category | flops | bytes accessed | tf_op | source)
XLA Modules:
  0.0 295.8 jit_solution(2267634805396735870)
XLA Ops:
  6.5 0.7 all-gather.2.cloned.1.call-update
  7.3 0.7 compare_select_fusion.2
  7.9 1.3 gather_fusion
  9.3 0.1 lt.96
  9.3 0.1 lt.97
  9.4 0.1 lt.98
  9.5 1.3 gather_fusion.1
  10.8 0.1 gather.22
  10.8 0.1 lt.94
  11.0 0.2 reduce_window_sum.17
  11.2 0.2 select_reduce_fusion
  11.4 0.1 reshape.695
  11.5 2.2 gather_fusion.2
  13.7 5.2 %all-to-all-start = ((bf16[64,128,128]{2,1,0:T(8,128)(2,1)}), bf16[64,128,128]{2,1,0:T(8,128)(2,1)S(1)}, u32[]{:S(2)}, u32[]{:S(2)}) async-start(bf16[64,128,128]{2,1,0:T(8,128)(2,1)} %gather_fusion.2), calls=%async_computation | async-start | bytes 4194304 | tf_op jit(solution)/shard_map/all_to_all | solution.py:97
  18.9 0.1 dynamic_slice.9
  19.0 0.1 copy.24
  19.2 0.1 copy.25
  19.4 0.6 fusion.107
  20.0 0.6 add_convert_fusion.2
  20.7 0.7 add_convert_fusion.3
  21.4 0.5 multiply_cosine_fusion.4
  21.9 0.2 subtract_convert_fusion
  22.2 0.2 reduce_window_sum.18
  22.4 0.2 copy.19
  22.6 0.2 tile.13
  22.8 0.1 copy.26
  23.0 3.7 %gather_fusion.4 = bf16[64,128,128]{2,1,0:T(8,128)(2,1)} fusion(bf16[64,128,128]{2,1,0:T(8,128)(2,1)} %param.13, s32[1024]{0:T(1024)S(1)} %pad_clamp_fusion.1), kind=kCustom, calls=%fused_computation.4 | custom fusion | bytes 4194560 | tf_op jit(solution)/shard_map/gather | solution.py:70
  26.7 0.2 copy.22
  26.9 0.7 iota_compare_fusion.3
  27.6 0.6 iota_compare_fusion.2
  28.2 0.6 select_reduce_fusion.1
  28.9 0.6 iota_convert_fusion
  29.5 1.9 fusion.82
  31.4 2.0 fusion.109
  33.4 1.9 fusion.108
  35.3 21.4 %all-to-all-done = bf16[64,128,128]{2,1,0:T(8,128)(2,1)S(1)} async-done(((bf16[64,128,128]{2,1,0:T(8,128)(2,1)}), bf16[64,128,128]{2,1,0:T(8,128)(2,1)S(1)}, u32[]{:S(2)}, u32[]{:S(2)}) %all-to-all-start) | async-done | bytes 2097184 | tf_op jit(solution)/shard_map/all_to_all | solution.py:97
  56.7 4.4 %all-to-all-start.1 = ((bf16[64,128,128]{2,1,0:T(8,128)(2,1)}), bf16[64,128,128]{2,1,0:T(8,128)(2,1)}, u32[]{:S(2)}, u32[]{:S(2)}) async-start(bf16[64,128,128]{2,1,0:T(8,128)(2,1)} %gather_fusion.4), calls=%async_computation.1 | async-start | bytes 4194304 | tf_op jit(solution)/shard_map/all_to_all | solution.py:98
  61.1 0.2 reduce-scatter.2.cloned.1.call-start
  61.3 2.2 gather_fusion.3
  63.5 1.7 fusion.104
  65.1 0.2 bitcast_convert_fusion
  65.4 0.2 bitcast_convert_fusion.1
  65.6 0.3 copy-done.12
  65.9 10.9 %fusion.45 = (bf16[4096,64]{1,0:T(8,128)(2,1)S(1)}, bf16[4096,64]{1,0:T(8,128)(2,1)S(1)}, bf16[4096,64]{1,0:T(8,128)(2,1)S(1)}, bf16[4096,64]{1,0:T(8,128)(2,1)}) fusion(f32[4096,1,128]{2,0,1:T(8,128)S(1)} %bitcast_convert_fusion.1, f32[64]{0:T(128)S(1)} %multiply_power_fusion, f32[4096]{0:T(1024)S(1)} %copy-done.12, f32[4096,1,128]{2,0,1:T(8,128)S(1)} %bitcast_convert_fusion), kind=kLoop, calls=%fused_computation.64 | loop fusion | flops 4456448 | bytes 6308096 | tf_op jit(solution)/shard_map/concatenate | solution.py:20
  76.7 3.0 %fusion = (f32[1024]{0:T(1024)S(1)}, f32[1024,4096]{1,0:T(8,128)S(1)}) fusion(pred[4096]{0:T(1024)(128)(4,1)S(1)} %iota_compare_fusion.3, bf16[1024,128]{1,0:T(8,128)(2,1)S(1)} %bitcast.88, bf16[4096,64]{1,0:T(8,128)(2,1)S(1)} %get-tuple-element.10, bf16[4096,64]{1,0:T(8,128)(2,1)S(1)} %get-tuple-element.9), kind=kOutput, calls=%fused_computation.10 | convolution fusion | flops 1088420864 | bytes 18096128 | tf_op jit(solution)/shard_map/qd,kd->qk/dot_general | solution.py:123
  79.8 0.2 fusion.46
  79.9 4.3 %fusion.2 = f32[1024]{0:T(1024)S(1)} fusion(f32[1024,4096]{1,0:T(8,128)S(1)} %get-tuple-element.46, f32[1024]{0:T(1024)S(1)} %max.16, pred[4096]{0:T(1024)(128)(4,1)S(1)} %iota_compare_fusion.3), kind=kLoop, calls=%fused_computation.12 | loop fusion | flops 16776192 | bytes 16789504 | tf_op jit(solution)/shard_map/reduce_sum | solution.py:132
  84.2 1.2 copy-done.2
  85.5 24.2 %all-to-all-done.1 = bf16[64,128,128]{2,1,0:T(8,128)(2,1)} async-done(((bf16[64,128,128]{2,1,0:T(8,128)(2,1)}), bf16[64,128,128]{2,1,0:T(8,128)(2,1)}, u32[]{:S(2)}, u32[]{:S(2)}) %all-to-all-start.1) | async-done | bytes 2097184 | tf_op jit(solution)/shard_map/all_to_all | solution.py:98
  109.7 2.5 gather_fusion.5
  112.2 1.2 fusion.105
  113.4 7.7 %fusion.8 = f32[1024,128]{1,0:T(8,128)S(1)} fusion(bf16[4096,128]{1,0:T(8,128)(2,1)S(1)} %bitcast.95, f32[1024,4096]{1,0:T(8,128)} %copy-done.2, f32[1024]{0:T(1024)S(1)} %max.16, pred[4096]{0:T(1024)(128)(4,1)S(1)} %iota_compare_fusion.3), kind=kOutput, calls=%fused_computation.18 | convolution fusion | flops 1090519040 | bytes 18358272 | tf_op jit(solution)/shard_map/dot_general | solution.py:135
  121.1 1.1 fusion.32
  122.2 1.1 copy.20
  123.3 2.9 fusion.1
  126.3 0.2 fusion.48
  126.5 4.5 %fusion.4 = f32[1024]{0:T(1024)S(1)} fusion(f32[1024,4096]{1,0:T(8,128)S(1)} %get-tuple-element.42, f32[1024]{0:T(1024)S(1)} %max.17, pred[4096]{0:T(1024)(128)(4,1)S(1)} %iota_compare_fusion.2), kind=kLoop, calls=%fused_computation.14 | loop fusion | flops 16776192 | bytes 16789504 | tf_op jit(solution)/shard_map/reduce_sum | solution.py:132
  131.1 3.3 %fusion.6 = f32[1024,128]{1,0:T(8,128)S(1)} fusion(bf16[4096,128]{1,0:T(8,128)(2,1)S(1)} %bitcast.94, f32[1024,4096]{1,0:T(8,128)S(1)} %get-tuple-element.42, f32[1024]{0:T(1024)S(1)} %max.17, pred[4096]{0:T(1024)(128)(4,1)S(1)} %iota_compare_fusion.2), kind=kOutput, calls=%fused_computation.17 | convolution fusion | flops 1090519040 | bytes 18358272 | tf_op jit(solution)/shard_map/dot_general | solution.py:135
  134.4 0.4 fusion.33
  134.7 0.1 copy.23
  134.9 0.0 all-gather.2.cloned.1.call-done
  134.9 10.2 %convolution_convert_fusion = bf16[512,8192]{1,0:T(8,128)(2,1)} fusion(bf16[512,8192]{1,0:T(8,128)(2,1)} %all-gather.2.cloned.1.call-done, bf16[256,512]{0,1:T(8,128)(2,1)S(1)} %bitcast.90, bf16[256,512]{0,1:T(8,128)(2,1)S(1)} %bitcast.89), kind=kOutput, calls=%fused_computation.16 | convolution fusion | flops 4300210176 | bytes 17301504 | tf_op jit(solution)/shard_map/dot_general | solution.py:150
  145.1 0.0 reduce-scatter.2.cloned.1.call-update
  145.1 143.8 %reduce-scatter.2.cloned.1.call-done = bf16[512,2048]{1,0:T(8,128)(2,1)} async-done(((bf16[512,8192]{1,0:T(8,128)(2,1)}), bf16[512,2048]{1,0:T(8,128)(2,1)}) %reduce-scatter.2.cloned.1.call-update) | async-done | bytes 2097168 | tf_op jit(solution)/shard_map/reduce_scatter | solution.py:156
  (69 shorter events, 0.4 us)
Async XLA Ops:
  6.5 5.0 %copy-start = (bf16[64,128,128]{2,1,0:T(8,128)(2,1)S(1)}, bf16[64,128,128]{2,1,0:T(8,128)(2,1)}, u32[]{:S(2)}) copy-start(bf16[64,128,128]{2,1,0:T(8,128)(2,1)} %param.12) | copy-start | bytes 6291460
  6.5 128.4 %all-gather.2.cloned.1.call-start = ((), (), s32[]{:S(2)}) async-start(), calls=%async_computation.3 | async-start | bytes 9437184 | tf_op jit(solution)/shard_map/all_gather | solution.py:152
  10.9 8.4 %copy-start.17 = (pred[8,64]{1,0:T(8,128)(4,1)}, pred[8,64]{1,0:T(8,128)(4,1)S(1)}, u32[]{:S(2)}) copy-start(pred[8,64]{1,0:T(8,128)(4,1)S(1)} %get-tuple-element.8) | copy-start | bytes 1540
  11.5 7.4 %copy-start.10 = (bf16[512,512]{1,0:T(8,128)(2,1)S(1)}, bf16[512,512]{1,0:T(8,128)(2,1)}, u32[]{:S(2)}) copy-start(bf16[512,512]{1,0:T(8,128)(2,1)} %param.9) | copy-start | bytes 1572868
  13.7 43.0 %all-to-all-start = ((bf16[64,128,128]{2,1,0:T(8,128)(2,1)}), bf16[64,128,128]{2,1,0:T(8,128)(2,1)S(1)}, u32[]{:S(2)}, u32[]{:S(2)}) async-start(bf16[64,128,128]{2,1,0:T(8,128)(2,1)} %gather_fusion.2), calls=%async_computation | async-start | bytes 4194304 | tf_op jit(solution)/shard_map/all_to_all | solution.py:97
  19.4 3.6 %copy-start.19 = (pred[64]{0:T(512)(128)(4,1)}, pred[64]{0:T(512)(128)(4,1)S(1)}, u32[]{:S(2)}) copy-start(pred[64]{0:T(512)(128)(4,1)S(1)} %fusion.92) | copy-start | bytes 196
  19.4 3.6 %copy-start.20 = (s32[64]{0:T(128)}, s32[64]{0:T(128)S(1)}, u32[]{:S(2)}) copy-start(s32[64]{0:T(128)S(1)} %fusion.93) | copy-start | bytes 772
  20.6 6.1 %copy-start.13 = (f32[256]{0:T(256)}, f32[256]{0:T(256)S(1)}, u32[]{:S(2)}) copy-start(f32[256]{0:T(256)S(1)} %add_convert_fusion.2) | copy-start | bytes 3076
  21.4 1.6 copy-start.14
  21.9 7.6 %copy-start.11 = (bf16[512,128]{1,0:T(8,128)(2,1)S(1)}, bf16[512,128]{1,0:T(8,128)(2,1)}, u32[]{:S(2)}) copy-start(bf16[512,128]{1,0:T(8,128)(2,1)} %param.10) | copy-start | bytes 393220
  22.1 6.8 %copy-start.18 = (pred[8,64]{1,0:T(8,128)(4,1)S(1)}, pred[8,64]{1,0:T(8,128)(4,1)}, u32[]{:S(2)}) copy-start(pred[8,64]{1,0:T(8,128)(4,1)} %copy-done.17) | copy-start | bytes 1540
  22.6 10.8 %copy-start.4 = (bf16[4,256,128]{2,1,0:T(8,128)(2,1)}, bf16[4,256,128]{2,1,0:T(8,128)(2,1)S(1)}, u32[]{:S(2)}) copy-start(bf16[4,256,128]{2,1,0:T(8,128)(2,1)S(1)} %copy.19) | copy-start | bytes 786436
  56.7 53.0 %all-to-all-start.1 = ((bf16[64,128,128]{2,1,0:T(8,128)(2,1)}), bf16[64,128,128]{2,1,0:T(8,128)(2,1)}, u32[]{:S(2)}, u32[]{:S(2)}) async-start(bf16[64,128,128]{2,1,0:T(8,128)(2,1)} %gather_fusion.4), calls=%async_computation.1 | async-start | bytes 4194304 | tf_op jit(solution)/shard_map/all_to_all | solution.py:98
  61.1 227.9 %reduce-scatter.2.cloned.1.call-start = ((), (), s32[]{:S(2)}) async-start(), calls=%async_computation.4 | async-start | bytes 10485760 | tf_op jit(solution)/shard_map/reduce_scatter | solution.py:156
  65.1 0.7 copy-start.12
  65.9 10.9 %copy-start.5 = (bf16[4,256,128]{2,1,0:T(8,128)(2,1)S(1)}, bf16[4,256,128]{2,1,0:T(8,128)(2,1)}, u32[]{:S(2)}) copy-start(bf16[4,256,128]{2,1,0:T(8,128)(2,1)} %copy-done.4) | copy-start | bytes 786436
  76.7 3.0 %copy-start.16 = (f32[1024]{0:T(1024)S(1)}, f32[1024]{0:T(1024)}, u32[]{:S(2)}) copy-start(f32[1024]{0:T(1024)} %get-tuple-element.47) | copy-start | bytes 12292
  76.7 3.0 %copy-start.7 = (f32[1024,256]{0,1:T(8,128)S(1)}, f32[1024,256]{0,1:T(8,128)}, u32[]{:S(2)}) copy-start(f32[1024,256]{0,1:T(8,128)} %get-tuple-element.48) | copy-start | bytes 3145732
  79.7 5.7 %copy-start.2 = (f32[1024,4096]{1,0:T(8,128)}, f32[1024,4096]{1,0:T(8,128)S(1)}, u32[]{:S(2)}) copy-start(f32[1024,4096]{1,0:T(8,128)S(1)} %get-tuple-element.46) | copy-start | bytes 50331652
  113.4 7.7 %copy-start.8 = (f32[1024,256]{0,1:T(8,128)S(1)}, f32[1024,256]{0,1:T(8,128)}, u32[]{:S(2)}) copy-start(f32[1024,256]{0,1:T(8,128)} %get-tuple-element.48) | copy-start | bytes 3145732
  113.4 7.7 %copy-start.21 = (bf16[512,128]{1,0:T(8,128)(2,1)S(1)}, bf16[512,128]{1,0:T(8,128)(2,1)}, u32[]{:S(2)}) copy-start(bf16[512,128]{1,0:T(8,128)(2,1)} %param.11) | copy-start | bytes 393220
  113.4 9.9 %copy-start.3 = (bf16[4096,64]{1,0:T(8,128)(2,1)S(1)}, bf16[4096,64]{1,0:T(8,128)(2,1)}, u32[]{:S(2)}) copy-start(bf16[4096,64]{1,0:T(8,128)(2,1)} %get-tuple-element.30) | copy-start | bytes 1572868
  123.3 3.0 %copy-start.15 = (f32[1024]{0:T(1024)S(1)}, f32[1024]{0:T(1024)}, u32[]{:S(2)}) copy-start(f32[1024]{0:T(1024)} %get-tuple-element.43) | copy-start | bytes 12292
  123.3 3.0 %copy-start.6 = (f32[1024,256]{0,1:T(8,128)S(1)}, f32[1024,256]{0,1:T(8,128)}, u32[]{:S(2)}) copy-start(f32[1024,256]{0,1:T(8,128)} %get-tuple-element.44) | copy-start | bytes 3145732
  126.5 4.6 %copy-start.9 = (bf16[32,128,128]{2,1,0:T(8,128)(2,1)S(1)}, bf16[32,128,128]{2,1,0:T(8,128)(2,1)}, u32[]{:S(2)}) copy-start(bf16[32,128,128]{2,1,0:T(8,128)(2,1)} %get-tuple-element.16) | copy-start | bytes 3145732
  131.0 3.3 %copy-start.22 = (bf16[512,128]{1,0:T(8,128)(2,1)S(1)}, bf16[512,128]{1,0:T(8,128)(2,1)}, u32[]{:S(2)}) copy-start(bf16[512,128]{1,0:T(8,128)(2,1)} %param.11) | copy-start | bytes 393220
  145.1 143.9 %copy-start.1 = (bf16[64,128,128]{2,1,0:T(8,128)(2,1)S(1)}, bf16[64,128,128]{2,1,0:T(8,128)(2,1)}, u32[]{:S(2)}) copy-start(bf16[64,128,128]{2,1,0:T(8,128)(2,1)} %param.12) | copy-start | bytes 6291460
Sparse Core Ops, SparseCore 0:
  9.3 100.8 all-gather.1
  145.3 143.6 reduce-scatter.1
where the time goes:
time: 296 us
  waiting for transfers between devices  190 us (64%)
  matrix products  32.5 us (11%)
  other arithmetic  28.4 us (10%)
  local copies, waits for them, and re-layouts  21 us (7%)
  between operations  14 us (5%)
  starting transfers between devices  9.77 us (3%)
    reduce_scatter x1, waiting for transfers between devices, local(): lax.psum_scatter(partial_value.astype(jnp.bfloat16), 'tp', scatter_dimens...  144 us
    all_to_all x1, waiting for transfers between devices, local(): lax.all_to_all(send_vals, 'pool', split_axis=0, concat_axis=0, tiled=True)  24.2 us
    all_to_all x1, waiting for transfers between devices, local(): lax.all_to_all(send_keys, 'pool', split_axis=0, concat_axis=0, tiled=True)  21.4 us
    concatenate x2, other arithmetic, rotate(): jnp.concatenate([lower_half * cosine - upper_half * sine_part, upper_half...  12.7 us
    dot_general x2, matrix products, local(): jnp.dot(far_weight.astype(jnp.bfloat16), hist_vals[seat_number], preferre...  11 us
    dot_general x1, matrix products, local(): jnp.dot(attended, lax.all_gather(out_weight, 'pool', axis=1, tiled=True),...  10.2 us
    reduce_sum x2, other arithmetic, local(): jnp.sum(far_weight, axis=1, keepdims=True)  8.82 us
    dot_general x2, matrix products, local(): jnp.einsum('qd,kd->qk', roped_query, roped_hist, preferred_element_type=j...  5.92 us
  transfers between devices with their start and end apart: 4, of which 3 were waited for; matrix products, arithmetic and copies ran while one was open for 24% of the time, Pallas kernels for 0%

commit v1 on v0

v1 whole, which is shorter than its diff:
```python
import functools
import math

import jax
import jax.numpy as jnp
import numpy as np
from jax import lax
from jax.experimental import pallas as pl
from jax.experimental.pallas import tpu as pltpu
from jax.sharding import PartitionSpec as P

rope_base = 1000000.0
MESH = pl.DeviceIdType.MESH
F32 = jnp.float32
BF16 = jnp.bfloat16
dot = functools.partial(jnp.dot, preferred_element_type=F32)


def kernel(
    pools,
    tps,
    seats,
    cap,
    meta_ref,
    tq_ref,
    tk_ref,
    tv_ref,
    cos_far,
    sin_far,
    cos_near,
    sin_near,
    send_k,
    send_v,
    weight,
    out_ref,
    keys,
    vals,
    gathered,
    attended,
    queries,
    scores,
    probs,
    flipped,
    acc,
    top,
    total,
    k_send,
    k_recv,
    v_send,
    v_recv,
    s_send,
    s_recv,
    g_send,
    g_recv,
    f_send,
    a_send,
    a_recv,
    local_sem,
):
    me = lax.axis_index("pool")
    row = lax.axis_index("tp")
    block = send_k.shape[1]
    head = send_k.shape[2]
    turn = tq_ref.shape[0] // seats
    group = tq_ref.shape[1] // head
    wide = group * turn
    chips = pools // 2
    share = pools // tps
    part = weight.shape[0] // pools
    w_cols = weight.shape[1]
    sibling = me + 1 - 2 * lax.rem(me, 2)
    core = lax.rem(me, 2)
    chip = me // 2
    target_row = me // share
    at_home = target_row == row

    barrier = pltpu.get_barrier_semaphore()

    def greet(pool_index, tp_index):
        pl.semaphore_signal(barrier, inc=1, device_id=(pool_index, tp_index), device_id_type=MESH)

    def greet_pool(i, carry):
        greet(lax.rem(me + i, pools), row)
        return carry

    lax.fori_loop(1, pools, greet_pool, 0)

    @pl.when(row > 0)
    def _():
        greet(me, row - 1)

    @pl.when(row < tps - 1)
    def _():
        greet(me, row + 1)

    def greet_source(i, carry):
        source_pool = row * share + i // tps
        source_row = lax.rem(i, tps)

        @pl.when(jnp.logical_not((source_pool == me) & (source_row == row)))
        def _():
            greet(source_pool, source_row)

        return carry

    lax.fori_loop(0, share * tps, greet_source, 0)
    greeted = (
        2 * pools
        - 1
        - at_home.astype(jnp.int32)
        + (row > 0).astype(jnp.int32)
        + (row < tps - 1).astype(jnp.int32)
    )
    pl.semaphore_wait(barrier, greeted)

    def kv_copies(q):
        rows = pl.ds(q * cap, cap)
        return (
            pltpu.make_async_remote_copy(
                src_ref=send_k.at[rows],
                dst_ref=keys.at[me],
                send_sem=k_send.at[q],
                recv_sem=k_recv.at[me],
                device_id=(q, row),
                device_id_type=MESH,
            ),
            pltpu.make_async_remote_copy(
                src_ref=send_v.at[rows],
                dst_ref=vals.at[me],
                send_sem=v_send.at[q],
                recv_sem=v_recv.at[me],
                device_id=(q, row),
                device_id_type=MESH,
            ),
        )

    def kv_arrival(s):
        return (
            pltpu.make_async_remote_copy(
                src_ref=keys.at[s],
                dst_ref=keys.at[s],
                send_sem=k_send.at[s],
                recv_sem=k_recv.at[s],
                device_id=(s, row),
                device_id_type=MESH,
            ),
            pltpu.make_async_remote_copy(
                src_ref=vals.at[s],
                dst_ref=vals.at[s],
                send_sem=v_send.at[s],
                recv_sem=v_recv.at[s],
                device_id=(s, row),
                device_id_type=MESH,
            ),
        )

    own_rows = pl.ds(me * cap, cap)
    own_k = pltpu.make_async_copy(send_k.at[own_rows], keys.at[me], local_sem.at[0])
    own_v = pltpu.make_async_copy(send_v.at[own_rows], vals.at[me], local_sem.at[1])
    own_k.start()
    own_v.start()

    def start_kv(i, carry):
        for copy in kv_copies(lax.rem(me + i, pools)):
            copy.start()
        return carry

    lax.fori_loop(1, pools, start_kv, 0)

    def scatter_copy(q):
        return pltpu.make_async_remote_copy(
            src_ref=weight.at[pl.ds(pl.multiple_of(q * part, part), part)],
            dst_ref=gathered.at[
                q,
                row,
                :,
                pl.ds(pl.multiple_of(lax.rem(me, share) * w_cols, w_cols), w_cols),
            ],
            send_sem=s_send.at[q],
            recv_sem=s_recv.at[lax.rem(me, share) * tps + row],
            device_id=(q, target_row),
            device_id_type=MESH,
        )

    own_w = pltpu.make_async_copy(
        weight.at[pl.ds(pl.multiple_of(me * part, part), part)],
        gathered.at[
            me, row, :, pl.ds(pl.multiple_of(lax.rem(me, share) * w_cols, w_cols), w_cols)
        ],
        local_sem.at[2],
    )

    def start_scatter(i, carry):
        q = lax.rem(me + i, pools)
        scatter_copy(q).start()
        return carry

    lax.fori_loop(1, pools, start_scatter, 0)

    @pl.when(at_home)
    def _():
        own_w.start()

    @pl.when(jnp.logical_not(at_home))
    def _():
        scatter_copy(me).start()

    def slab_copy(slab, pool_index, send_sem):
        return pltpu.make_async_remote_copy(
            src_ref=gathered.at[slab],
            dst_ref=gathered.at[slab],
            send_sem=send_sem,
            recv_sem=g_recv.at[slab],
            device_id=(pool_index, row),
            device_id_type=MESH,
        )

    def chip_peer(i):
        return lax.rem(chip + i, chips) * 2 + core

    def chip_source(i):
        return lax.rem(chip + chips - i, chips) * 2 + core

    def start_gather():
        def wait_piece(i, carry):
            piece_pool = row * share + i // tps
            piece_row = lax.rem(i, tps)

            @pl.when(jnp.logical_not((piece_pool == me) & (piece_row == row)))
            def _():
                landing = gathered.at[
                    me,
                    piece_row,
                    :,
                    pl.ds(pl.multiple_of((i // tps) * w_cols, w_cols), w_cols),
                ]
                pltpu.make_async_remote_copy(
                    src_ref=landing,
                    dst_ref=landing,
                    send_sem=s_send.at[0],
                    recv_sem=s_recv.at[i],
                    device_id=(piece_pool, piece_row),
                    device_id_type=MESH,
                ).wait_recv()

            return carry

        lax.fori_loop(0, share * tps, wait_piece, 0)

        @pl.when(at_home)
        def _():
            own_w.wait()

        def start_slab(i, carry):
            peer = chip_peer(i)
            slab_copy(me, peer, g_send.at[i]).start()
            return carry

        lax.fori_loop(1, chips, start_slab, 0)
        slab_copy(me, sibling, g_send.at[0]).start()

    def pass_on(i):
        slab = chip_source(i)
        copy = slab_copy(slab, sibling, f_send.at[i])
        copy.wait_recv()
        copy.start()

    factor = math.log2(math.e) / math.sqrt(head)
    tables = []
    for e in range(seats):
        far = cos_far.shape[0] - seats + e
        ca, sa = cos_far[far : far + 1, :], sin_far[far : far + 1, :]
        cb, sb = cos_near[...], sin_near[...]
        tables.append((ca * cb - sa * sb, sa * cb + ca * sb))

    def rope(x, cosine, sine):
        return x * cosine + pltpu.roll(x, head // 2, 1) * sine

    lanes = lax.broadcasted_iota(jnp.int32, (turn, wide), 1)
    unseen = lax.broadcasted_iota(jnp.int32, (turn, wide), 0) > lax.rem(lanes, turn)
    for e in range(seats):
        cosine, sine = tables[e]
        rows = slice(e * turn, (e + 1) * turn)
        for h in range(group):
            x = tq_ref[rows, h * head : (h + 1) * head].astype(F32)
            turned = rope(x, cosine, sine) * factor
            queries[e, :, h * turn : (h + 1) * turn] = turned.T.astype(BF16)
        new_keys = rope(tk_ref[rows, :].astype(F32), cosine, sine).astype(BF16)
        s = jnp.where(unseen, -jnp.inf, dot(new_keys, queries[e]))
        best = jnp.max(s, axis=0, keepdims=True)
        p = jnp.exp2(s - best)
        top[e : e + 1, :] = best
        total[e : e + 1, :] = jnp.sum(p, axis=0, keepdims=True)
        flipped_new = tv_ref[rows, :].astype(F32).T.astype(BF16)
        acc[e * head : (e + 1) * head, :] = dot(flipped_new, p.astype(BF16))

    depth = lax.broadcasted_iota(jnp.int32, (block, 1), 0)

    def attend(source):
        tops = [top[e : e + 1, :] for e in range(seats)]
        owners = []
        for b in range(cap):
            at = source * cap + b
            far, seat, limit = meta_ref[0, at], meta_ref[1, at], meta_ref[2, at]
            owners.append(seat)
            ca, sa = cos_far[pl.ds(far, 1), :], sin_far[pl.ds(far, 1), :]
            cb, sb = cos_near[0:block, :], sin_near[0:block, :]
            x = keys[source, b].astype(F32)
            turned = rope(x, ca * cb - sa * sb, sa * cb + ca * sb).astype(BF16)
            s = jnp.where(depth < limit, dot(turned, queries[seat]), -jnp.inf)
            scores[b * block : (b + 1) * block, :] = s
            best = jnp.max(s, axis=0, keepdims=True)
            upright = vals[source, b].astype(F32).T
            for e in range(seats):
                tops[e] = jnp.maximum(tops[e], jnp.where(seat == e, best, -jnp.inf))
                flipped[e * head : (e + 1) * head, b * block : (b + 1) * block] = jnp.where(
                    seat == e, upright, 0.0
                ).astype(BF16)
        alphas = [jnp.exp2(top[e : e + 1, :] - tops[e]) for e in range(seats)]
        sums = [total[e : e + 1, :] * alphas[e] for e in range(seats)]
        for b in range(cap):
            span = slice(b * block, (b + 1) * block)
            base = tops[0]
            for e in range(1, seats):
                base = jnp.where(owners[b] == e, tops[e], base)
            p = jnp.exp2(scores[span, :] - base)
            added = jnp.sum(p, axis=0, keepdims=True)
            for e in range(seats):
                sums[e] = sums[e] + jnp.where(owners[b] == e, added, 0.0)
            probs[span, :] = p.astype(BF16)
        gained = dot(flipped[...], probs[...])
        for e in range(seats):
            rows = slice(e * head, (e + 1) * head)
            acc[rows, :] = acc[rows, :] * alphas[e] + gained[rows, :]
            top[e : e + 1, :] = tops[e]
            total[e : e + 1, :] = sums[e]

    def step(i, carry):
        source = lax.rem(me + pools - i, pools)

        @pl.when(i == 0)
        def _():
            own_k.wait()
            own_v.wait()

        @pl.when(i > 0)
        def _():
            for copy in kv_arrival(source):
                copy.wait_recv()

        @pl.when(i == pools - 2)
        def _():
            start_gather()

        attend(source)
        return carry

    lax.fori_loop(0, pools, step, 0)

    for e in range(seats):
        rows = slice(e * turn, (e + 1) * turn)
        final = acc[e * head : (e + 1) * head, :] / total[e : e + 1, :]
        for h in range(group):
            attended[row, rows, h * head : (h + 1) * head] = (
                final[:, h * turn : (h + 1) * turn].T.astype(BF16)
            )

    def slot_copy(slot, neighbour, way, hop):
        return pltpu.make_async_remote_copy(
            src_ref=attended.at[slot],
            dst_ref=attended.at[slot],
            send_sem=a_send.at[way, hop],
            recv_sem=a_recv.at[slot],
            device_id=(me, neighbour),
            device_id_type=MESH,
        )

    def hop_sends(hop, act):
        @pl.when((row - hop >= 0) & (row < tps - 1))
        def _():
            act(slot_copy(row - hop, row + 1, 0, hop))

        @pl.when((row + hop < tps) & (row > 0))
        def _():
            act(slot_copy(row + hop, row - 1, 1, hop))

    def hop_waits(hop):
        @pl.when(row - hop >= 0)
        def _():
            slot_copy(row - hop, row - 1, 0, 0).wait_recv()

        @pl.when(row + hop < tps)
        def _():
            slot_copy(row + hop, row + 1, 1, 0).wait_recv()

    hop_sends(0, lambda copy: copy.start())
    passed = 1
    for hop in range(1, tps):
        hop_waits(hop)
        if hop < tps - 1:
            hop_sends(hop, lambda copy: copy.start())
        if passed < chips:
            pass_on(passed)
            passed += 1

    def rest(i, carry):
        pass_on(i)
        return carry

    lax.fori_loop(passed, chips, rest, 0)

    slab_copy(sibling, sibling, g_send.at[0]).wait_recv()

    def wait_passed(i, carry):
        slab = chip_source(i) - core + lax.rem(sibling, 2)
        slab_copy(slab, sibling, g_send.at[0]).wait_recv()
        return carry

    lax.fori_loop(1, chips, wait_passed, 0)

    tile = 256

    def project(n, carry):
        cols = pl.ds(pl.multiple_of(n * tile, tile), tile)
        result = jnp.zeros((out_ref.shape[0], tile), F32)
        for t in range(tps):
            w = gathered[:, t, :, cols].reshape(pools * part, tile)
            result = result + dot(attended[t], w)
        out_ref[:, cols] = result.astype(BF16)
        return carry

    lax.fori_loop(0, out_ref.shape[1] // tile, project, 0)

    def wait_sends(i, carry):
        q = lax.rem(me + i, pools)
        for copy in kv_copies(q):
            copy.wait_send()
        scatter_copy(q).wait_send()
        return carry

    lax.fori_loop(1, pools, wait_sends, 0)

    @pl.when(jnp.logical_not(at_home))
    def _():
        scatter_copy(me).wait_send()

    def wait_slabs(i, carry):
        slab_copy(me, chip_peer(i), g_send.at[i]).wait_send()
        slab_copy(chip_source(i), sibling, f_send.at[i]).wait_send()
        return carry

    lax.fori_loop(1, chips, wait_slabs, 0)
    slab_copy(me, sibling, g_send.at[0]).wait_send()
    for hop in range(tps - 1):
        hop_sends(hop, lambda copy: copy.wait_send())


def local(
    turn_query,
    turn_key,
    turn_value,
    pool_keys,
    pool_values,
    seat_session,
    history_len,
    block_map,
    out_weight,
):
    pools = lax.axis_size("pool")
    tps = lax.axis_size("tp")
    me = lax.axis_index("pool")
    blocks_here, block, head = pool_keys.shape
    block_count = block_map.shape[1]
    seats = seat_session.shape[0] // pools
    cap = seats * block_count // pools
    count = seats * block_count
    rows, width = turn_query.shape
    turn = rows // seats
    group = width // head
    wide = group * turn
    part = out_weight.shape[0] // pools
    out_cols = out_weight.shape[1] * pools // tps

    seat_length = history_len[seat_session]
    seat_map = block_map[seat_session]
    home = (seat_map // blocks_here).reshape(pools, count)
    slot = (seat_map % blocks_here).reshape(pools, count)
    numbers = jnp.arange(block_count, dtype=jnp.int32)
    alive = (numbers[None, :] * block < seat_length[:, None]).reshape(pools, count)
    ranks = jnp.arange(cap, dtype=jnp.int32)
    leaving = alive & (home == me)
    send_rank = jnp.cumsum(leaving.astype(jnp.int32), axis=1) - 1
    chosen = leaving[:, None, :] & (send_rank[:, None, :] == ranks[None, :, None])
    slot_table = jnp.sum(jnp.where(chosen, slot[:, None, :], 0), axis=2).reshape(pools * cap)
    send_keys = pool_keys[slot_table]
    send_vals = pool_values[slot_table]

    own_home = lax.dynamic_slice_in_dim(home, me, 1, 0)
    own_alive = lax.dynamic_slice_in_dim(alive, me, 1, 0)
    own_lengths = lax.dynamic_slice_in_dim(seat_length, me * seats, seats, 0)
    coming = own_alive & (own_home == jnp.arange(pools, dtype=jnp.int32)[:, None])
    coming_rank = jnp.cumsum(coming.astype(jnp.int32), axis=1) - 1
    landed = coming[:, None, :] & (coming_rank[:, None, :] == ranks[None, :, None])
    landed = landed.reshape(pools * cap, count)
    entry_number = jnp.tile(numbers, seats)
    entry_seat = jnp.repeat(jnp.arange(seats, dtype=jnp.int32), block_count)
    entry_limit = jnp.repeat(own_lengths, block_count) - entry_number * block
    meta = jnp.stack(
        [
            jnp.sum(jnp.where(landed, entry[None, :], 0), axis=1)
            for entry in (entry_number, entry_seat, entry_limit)
        ]
    )

    half = head // 2
    inverse = rope_base ** (-2.0 * np.arange(half) / head)
    inverse = np.concatenate([inverse, inverse])
    signs = np.concatenate([-np.ones(half), np.ones(half)])
    near = np.arange(turn)[:, None] * inverse[None, :]
    far = (np.arange(block_count) * block)[:, None] * inverse[None, :]
    cos_near = jnp.asarray(np.cos(near), F32)
    sin_near = jnp.asarray(np.sin(near) * signs, F32)
    start = own_lengths.astype(F32)[:, None] * jnp.asarray(inverse, F32)[None, :]
    cos_far = jnp.concatenate([jnp.asarray(np.cos(far), F32), jnp.cos(start)], axis=0)
    sin_far = jnp.concatenate(
        [jnp.asarray(np.sin(far) * signs, F32), jnp.sin(start) * jnp.asarray(signs, F32)], axis=0
    )

    in_vmem = pl.BlockSpec(memory_space=pltpu.VMEM)
    anywhere = pl.BlockSpec(memory_space=pl.ANY)
    dma = pltpu.SemaphoreType.DMA
    chips = pools // 2
    return pl.pallas_call(
        functools.partial(kernel, pools, tps, seats, cap),
        out_shape=jax.ShapeDtypeStruct((rows, out_cols), BF16),
        in_specs=[pl.BlockSpec(memory_space=pltpu.SMEM)] + [in_vmem] * 7 + [anywhere] * 3,
        out_specs=in_vmem,
        scratch_shapes=[
            pltpu.VMEM((pools, cap, block, head), BF16),
            pltpu.VMEM((pools, cap, block, head), BF16),
            pltpu.VMEM((pools, tps, part, out_cols), BF16),
            pltpu.VMEM((tps, rows, width), BF16),
            pltpu.VMEM((seats, head, wide), BF16),
            pltpu.VMEM((cap * block, wide), F32),
            pltpu.VMEM((cap * block, wide), BF16),
            pltpu.VMEM((seats * head, cap * block), BF16),
            pltpu.VMEM((seats * head, wide), F32),
            pltpu.VMEM((seats, wide), F32),
            pltpu.VMEM((seats, wide), F32),
            dma((pools,)),
            dma((pools,)),
            dma((pools,)),
            dma((pools,)),
            dma((pools,)),
            dma((pools,)),
            dma((chips,)),
            dma((pools,)),
            dma((chips,)),
            dma((2, tps)),
            dma((tps,)),
            dma((3,)),
        ],
        compiler_params=pltpu.CompilerParams(
            collective_id=0, has_side_effects=True, vmem_limit_bytes=56 * 1024 * 1024
        ),
    )(
        meta,
        turn_query,
        turn_key,
        turn_value,
        cos_far,
        sin_far,
        cos_near,
        sin_near,
        send_keys,
        send_vals,
        out_weight,
    )


def solution(mesh):
    return jax.shard_map(
        local,
        mesh=mesh,
        in_specs=(
            P("pool", "tp"),
            P("pool", "tp"),
            P("pool", "tp"),
            P("pool", None, "tp"),
            P("pool", None, "tp"),
            P(),
            P(),
            P(),
            P("tp", "pool"),
        ),
        out_specs=P("pool", "tp"),
        check_vma=False,
    )
```

time: 296 us -> 170 us (0.57)
  the two profiles are of different devices: /device:TPU:0 before, /device:TPU:25 now
where the time goes in v1:
time: 170 us
  Pallas kernels  152 us (89%)
  local copies, waits for them, and re-layouts  12.7 us (7%)
  other arithmetic  4.84 us (3%)
    pallas_call x1, Pallas kernels, local(): pl.pallas_call(functools.partial(kernel, pools, tps, seats, cap), out_sha...  152 us
    gather x1, local copies, waits for them, and re-layouts, local(): send_keys = pool_keys[slot_table]  3.72 us

profile of v1, /device:TPU:25, one launch (start us, length us, event | category | flops | bytes accessed | tf_op | source)
XLA Modules:
  0.0 169.7 jit_solution(10915615440691114151)
XLA Ops:
  0.0 0.0 copy-start
  0.0 0.8 compare_select_fusion.1
  0.8 0.1 lt.59
  0.9 0.1 broadcast_in_dim.70
  1.0 0.1 broadcast_in_dim.66
  1.1 1.3 gather_fusion
  2.4 0.1 fusion.9
  2.5 0.1 broadcast_in_dim.72
  2.6 0.1 reshape.293
  2.6 0.8 fusion.5
  3.4 0.1 lt.62
  3.5 0.1 lt.63
  3.6 0.1 lt.64
  3.7 1.3 gather_fusion.1
  4.9 0.1 gather.16
  5.0 0.2 reduce_window_sum.18
  5.3 0.2 select_reduce_fusion
  5.5 0.1 reshape.294
  5.6 0.2 reduce_window_sum.17
  5.8 0.5 select_reduce_fusion.3
  6.3 0.1 stack.12
  6.4 0.1 stack.14
  6.5 0.1 stack.13
  6.6 0.6 pad_add_fusion.meta_ref
  7.2 1.4 pad_maximum_fusion
  8.5 0.0 copy-done
  8.5 2.2 %gather_fusion.3 = bf16[64,128,128]{2,1,0:T(8,128)(2,1)} fusion(bf16[64,128,128]{2,1,0:T(8,128)(2,1)S(1)} %copy-done, s32[1024]{0:T(1024)S(1)} %pad_clamp_fusion), kind=kCustom, calls=%fused_computation.3 | custom fusion | bytes 4194560 | tf_op jit(solution)/shard_map/gather | solution.py:496
  10.7 3.7 %gather_fusion.2 = bf16[64,128,128]{2,1,0:T(8,128)(2,1)} fusion(bf16[64,128,128]{2,1,0:T(8,128)(2,1)} %param.18, s32[1024]{0:T(1024)S(1)} %pad_clamp_fusion), kind=kCustom, calls=%fused_computation.2 | custom fusion | bytes 4194560 | tf_op jit(solution)/shard_map/gather | solution.py:495
  14.4 152.1 %shard_map.145 = bf16[512,2048]{1,0:T(8,128)(2,1)} custom-call(s32[3,64]{1,0:T(4,128)} %pad_add_fusion.meta_ref, bf16[512,512]{1,0:T(8,128)(2,1)} %tq_ref.1, bf16[512,128]{1,0:T(8,128)(2,1)} %tk_ref.1, bf16[512,128]{1,0:T(8,128)(2,1)} %tv_ref.1, f32[34,128]{1,0:T(8,128)} %get-tuple-element.18.cos_far, f32[34,128]{1,0:T(8,128)} %get-tuple-element.19.sin_far, ...), custom_call_target="tpu_custom_call" | custom-call | tf_op jit(solution)/shard_map/pallas_call | solution.py:533
  166.5 3.2 %copy.17 = bf16[512,2048]{1,0:T(8,128)(2,1)} copy(bf16[512,2048]{1,0:T(8,128)(2,1)} %shard_map.145) | data formatting | bytes 4194304
  (14 shorter events, 0.1 us)
Async XLA Ops:
  0.0 8.5 %copy-start = (bf16[64,128,128]{2,1,0:T(8,128)(2,1)S(1)}, bf16[64,128,128]{2,1,0:T(8,128)(2,1)}, u32[]{:S(2)}) copy-start(bf16[64,128,128]{2,1,0:T(8,128)(2,1)} %param.19) | copy-start | bytes 6291460
